TPU v7x, 128 devices: a whole 4x4x4 slice. The times are simulated.
128 devices in a mesh: dp: 128 (over x, z, y, core).
Axes of the slice: x: 4, y: 4, z: 4, core: 2. Of those that a mesh axis runs over, the one named last changes fastest.
Arguments:
- text_input: bfloat16 [49152, 768], P('dp'), may hold values from -24 to 24
- caption_lengths: int32 [768, 4], P('dp'), may hold values from 4 to 16, as said below
- image_tokens: bfloat16 [153600, 768], P('dp'), may hold values from -6 to 6
- image_attn: bfloat16 [768, 3072], replicated, may hold values from -0.21875 to 0.21875
- image_mlp: bfloat16 [2, 768, 3072], replicated, may hold values from -0.21875 to 0.21875
- image_vectors: float32 [12, 768], replicated, may hold values from -1.5 to 2.5
- attn_master: float32 [768, 3072], P('dp'), may hold values from -0.21875 to 0.21875
- mlp_master: float32 [2, 768, 3072], P(None, 'dp'), may hold values from -0.21875 to 0.21875
- vector_master: float32 [12, 768], P(None, 'dp'), may hold values from -1.5 to 2.5
- attn_first: float32 [768, 3072], P('dp'), may hold values from -2.3841858e-06 to 2.3841858e-06
- mlp_first: float32 [2, 768, 3072], P(None, 'dp'), may hold values from -2.3841858e-06 to 2.3841858e-06
- vector_first: float32 [12, 768], P(None, 'dp'), may hold values from -9.536743e-06 to 9.536743e-06
- attn_second: float32 [768, 3072], P('dp'), may hold values from 1.4110136e-14 to 5.6440543e-14
- mlp_second: float32 [2, 768, 3072], P(None, 'dp'), may hold values from 1.4110136e-14 to 5.6440543e-14
- vector_second: float32 [12, 768], P(None, 'dp'), may hold values from 1.4110136e-13 to 5.6440546e-13
Outputs:
- input_grad: float32 [49152, 768], P('dp')
- grad_norm: float32 [], replicated
- attn_grad: float32 [768, 3072], P('dp')
- mlp_grad: float32 [2, 768, 3072], P(None, 'dp')
- vector_grad: float32 [12, 768], P(None, 'dp')
- attn_first_new: float32 [768, 3072], P('dp')
- mlp_first_new: float32 [2, 768, 3072], P(None, 'dp')
- vector_first_new: float32 [12, 768], P(None, 'dp')
- attn_second_new: float32 [768, 3072], P('dp')
- mlp_second_new: float32 [2, 768, 3072], P(None, 'dp')
- vector_second_new: float32 [12, 768], P(None, 'dp')
- attn_new: float32 [768, 3072], P('dp')
- mlp_new: float32 [2, 768, 3072], P(None, 'dp')
- vector_new: float32 [12, 768], P(None, 'dp')
Inputs may be any that keep to these rules, and one draw needn't show every extreme that they name: `caption_lengths`: 4 caption lengths for each text row of 64 tokens; a row's positions past their sum are padding.
All inputs are finite; a program needn't handle non-finite values.
Results may differ from a plain program's by a relative error of at most 0.023.
Values may be sent and summed in bfloat16 or wider, within the bound.
A program may use at most 192 MiB of HBM per device.

v0:
```python
import jax
import jax.numpy as jnp
from jax import lax
from jax.sharding import PartitionSpec as P

STEP = 10


logit_scale = 60.0
clip_norm = 0.01
learn_rate = 0.05
vector_rate = 0.3
beta_first = 0.9
beta_second = 0.999
adam_epsilon = 1e-08
weight_decay = 0.1
bfloat = jnp.bfloat16
single = jnp.float32


def layer_norm(values, gain_row, bias_row):
    center = jnp.mean(values, -1, keepdims=True)
    shifted = values - center
    spread = jnp.mean(shifted * shifted, -1, keepdims=True)
    return shifted * lax.rsqrt(spread + 1e-06) * gain_row + bias_row


def unit_rows(values):
    return values * lax.rsqrt(jnp.sum(values * values, -1, keepdims=True) + 1e-06)


def log_sum_exp(values, axis_index):
    maximum = jnp.max(values, axis_index, keepdims=True)
    return jnp.log(jnp.sum(jnp.exp(values - maximum), axis_index)) + jnp.squeeze(
        maximum, axis_index
    )


def caption_slots(lengths, row_len):
    row_ends = jnp.cumsum(lengths, axis=1)
    position = jnp.arange(row_len, dtype=jnp.int32)
    return jnp.sum((position[None, :, None] >= row_ends[:, None, :]).astype(jnp.int32), -1)


def pool_matrix(lengths, slot_ids):
    row_count, slot_count = lengths.shape
    row_base = slot_count * jnp.arange(row_count, dtype=jnp.int32)[:, None]
    owner_pair = jnp.where(slot_ids < slot_count, slot_ids + row_base, -1).reshape(-1)
    target = jnp.arange(row_count * slot_count, dtype=jnp.int32)
    member = (owner_pair[:, None] == target[None, :]).astype(single)
    return member / lengths.reshape(-1).astype(single)[None, :]


def attention_logits(queries, key_rows, allowed):
    scores = jnp.einsum("nqhd,nkhd->nhqk", queries, key_rows, preferred_element_type=single)
    return jnp.where(allowed[:, None], scores * 0.125, -1e30)


def block_forward(inputs, attn_weight, mlp_weight, vectors, allowed):
    sequences, length, features = inputs.shape
    head_count = features // 64
    tokens_flat = inputs.reshape(sequences * length, features)
    normed = layer_norm(tokens_flat, vectors[0], vectors[1]).astype(bfloat)
    biases = jnp.concatenate([vectors[4], jnp.zeros_like(vectors[4]), vectors[5]])
    triple = jnp.dot(normed, attn_weight[:, : 3 * features], preferred_element_type=single) + biases
    projected = triple.astype(bfloat).reshape(sequences, length, 3, head_count, 64)
    logits = attention_logits(projected[:, :, 0], projected[:, :, 1], allowed)
    maximum = jnp.max(logits, -1, keepdims=True)
    weights = jnp.exp(logits - maximum)
    totals = jnp.sum(weights, -1, keepdims=True)
    attn_probs = (weights / totals).astype(bfloat)
    log_totals = maximum + jnp.log(totals)
    attended = jnp.einsum(
        "nhqk,nkhd->nqhd", attn_probs, projected[:, :, 2], preferred_element_type=single
    )
    attended = attended.reshape(sequences * length, features).astype(bfloat)
    residual = (
        tokens_flat
        + jnp.dot(attended, attn_weight[:, 3 * features :], preferred_element_type=single)
        + vectors[6]
    )
    normed_two = layer_norm(residual, vectors[2], vectors[3]).astype(bfloat)
    hidden = jnp.dot(normed_two, mlp_weight[0], preferred_element_type=single) + vectors[
        8:
    ].reshape(-1)
    active = jax.nn.gelu(hidden).astype(bfloat)
    output = (
        residual
        + jnp.einsum("tf,df->td", active, mlp_weight[1], preferred_element_type=single)
        + vectors[7]
    )
    saved_state = (
        tokens_flat,
        normed,
        projected,
        log_totals,
        attended,
        residual,
        normed_two,
        hidden,
        active,
    )
    return (output, saved_state)


def block_backward(upstream, saved_state, attn_weight, mlp_weight, vectors, allowed):
    tokens_flat, normed, projected, log_totals, attended, residual, normed_two, hidden, active = (
        saved_state
    )
    features = tokens_flat.shape[1]
    sequences, seq_len, head_count = (projected.shape[0], projected.shape[1], projected.shape[3])
    branch_two = upstream.astype(bfloat)
    down_grad = jnp.einsum("td,tf->df", branch_two, active, preferred_element_type=single)
    down_bias = jnp.sum(branch_two.astype(single), 0)
    active_grad = jnp.dot(branch_two, mlp_weight[1], preferred_element_type=single)
    unused, gelu_back = jax.vjp(jax.nn.gelu, hidden)
    hidden_grad = gelu_back(active_grad)[0].astype(bfloat)
    up_grad = jnp.einsum("td,tf->df", normed_two, hidden_grad, preferred_element_type=single)
    up_bias = jnp.sum(hidden_grad.astype(single), 0)
    normed_grad = jnp.einsum("tf,df->td", hidden_grad, mlp_weight[0], preferred_element_type=single)
    unused, second_back = jax.vjp(layer_norm, residual, vectors[2], vectors[3])
    resid_part, gain_two, shift_two = second_back(normed_grad)
    resid_grad = upstream + resid_part
    branch_one = resid_grad.astype(bfloat)
    out_grad = jnp.einsum("td,te->de", attended, branch_one, preferred_element_type=single)
    out_bias = jnp.sum(branch_one.astype(single), 0)
    attended_grad = jnp.einsum(
        "te,de->td", branch_one, attn_weight[:, 3 * features :], preferred_element_type=single
    )
    attended_grad = attended_grad.astype(bfloat).reshape(sequences, seq_len, head_count, 64)
    queries, key_rows, value_rows = (projected[:, :, 0], projected[:, :, 1], projected[:, :, 2])
    attn_probs = jnp.exp(attention_logits(queries, key_rows, allowed) - log_totals)
    value_grad = jnp.einsum(
        "nhqk,nqhd->nkhd", attn_probs.astype(bfloat), attended_grad, preferred_element_type=single
    )
    prob_grad = jnp.einsum(
        "nqhd,nkhd->nhqk", attended_grad, value_rows, preferred_element_type=single
    )
    score_grad = (
        attn_probs * (prob_grad - jnp.sum(attn_probs * prob_grad, -1, keepdims=True)) * 0.125
    )
    score_grad = score_grad.astype(bfloat)
    query_grad = jnp.einsum("nhqk,nkhd->nqhd", score_grad, key_rows, preferred_element_type=single)
    key_grad = jnp.einsum("nhqk,nqhd->nkhd", score_grad, queries, preferred_element_type=single)
    triple_grad = (
        jnp.stack([query_grad, key_grad, value_grad], 2).astype(bfloat).reshape(-1, 3 * features)
    )
    qkv_grad = jnp.einsum("td,te->de", normed, triple_grad, preferred_element_type=single)
    triple_bias = jnp.sum(triple_grad.astype(single), 0)
    first_grad = jnp.einsum(
        "te,de->td", triple_grad, attn_weight[:, : 3 * features], preferred_element_type=single
    )
    unused, first_back = jax.vjp(layer_norm, tokens_flat, vectors[0], vectors[1])
    input_part, gain_one, shift_one = first_back(first_grad)
    input_grad = resid_grad + input_part
    attn_grad = jnp.concatenate([qkv_grad, out_grad], 1)
    mlp_grad = jnp.stack([up_grad, down_grad])
    vector_rows = jnp.stack(
        [
            gain_one,
            shift_one,
            gain_two,
            shift_two,
            triple_bias[:features],
            triple_bias[2 * features :],
            out_bias,
            down_bias,
        ]
    )
    vector_grad = jnp.concatenate([vector_rows, up_bias.reshape(4, features)], 0)
    return (input_grad, attn_grad, mlp_grad, vector_grad)


def sum_squares(arrays):
    return sum((jnp.sum(member * member) for member in arrays))


def adam_update(weight, gradient, first_moment, second_moment, factor, rate, decay_rate):
    clipped = gradient * factor
    first_new = beta_first * first_moment + (1.0 - beta_first) * clipped
    second_new = beta_second * second_moment + (1.0 - beta_second) * clipped * clipped
    ratio = (
        first_new
        / (1.0 - beta_first**STEP)
        / (jnp.sqrt(second_new / (1.0 - beta_second**STEP)) + adam_epsilon)
    )
    return (first_new, second_new, weight - rate * (ratio + decay_rate * weight))


def shards(
    text_input,
    caption_lengths,
    image_tokens,
    image_attn,
    image_mlp,
    image_vectors,
    attn_master,
    mlp_master,
    vector_master,
    attn_first,
    mlp_first,
    vector_first,
    attn_second,
    mlp_second,
    vector_second,
):
    attn_weight, mlp_weight, vector_low = (
        lax.all_gather(attn_master.astype(bfloat), "dp", axis=0, tiled=True),
        lax.all_gather(mlp_master.astype(bfloat), "dp", axis=1, tiled=True),
        lax.all_gather(vector_master.astype(bfloat), "dp", axis=1, tiled=True),
    )
    vectors = vector_low.astype(single)
    features = text_input.shape[1]
    row_count, slot_count = caption_lengths.shape
    row_len = text_input.shape[0] // row_count
    pair_count = row_count * slot_count
    patches = image_tokens.shape[0] // pair_count
    full_mask = jnp.ones((pair_count, patches, patches), jnp.bool_)
    image_inputs = image_tokens.astype(single).reshape(pair_count, patches, features)
    image_out, unused = block_forward(image_inputs, image_attn, image_mlp, image_vectors, full_mask)
    image_unit = unit_rows(jnp.mean(image_out.reshape(pair_count, patches, features), 1)).astype(
        bfloat
    )
    slot_ids = caption_slots(caption_lengths, row_len)
    allowed = slot_ids[:, :, None] == slot_ids[:, None, :]
    text_inputs = text_input.astype(single).reshape(row_count, row_len, features)
    text_out, saved_state = block_forward(text_inputs, attn_weight, mlp_weight, vectors, allowed)
    pooling = pool_matrix(caption_lengths, slot_ids)
    text_pooled = jnp.einsum("tj,td->jd", pooling, text_out, precision=lax.Precision.HIGHEST)
    text_unit = unit_rows(text_pooled).astype(bfloat)
    image_all, text_all = (
        lax.all_gather(image_unit, "dp", axis=0, tiled=True),
        lax.all_gather(text_unit, "dp", axis=0, tiled=True),
    )
    pair_total = pair_count * lax.axis_size("dp")
    offset = lax.axis_index("dp") * pair_count
    row_logits = logit_scale * jnp.einsum(
        "id,jd->ij", image_unit, text_all, preferred_element_type=single
    )
    row_totals = log_sum_exp(row_logits, 1)
    col_logits = logit_scale * jnp.einsum(
        "id,jd->ij", image_all, text_unit, preferred_element_type=single
    )
    col_totals = log_sum_exp(col_logits, 0)
    every_total = lax.all_gather(row_totals, "dp", axis=0, tiled=True)
    identity_part = (
        jnp.arange(pair_total, dtype=jnp.int32)[:, None]
        == offset + jnp.arange(pair_count, dtype=jnp.int32)[None, :]
    ).astype(single)
    row_probs = jnp.exp(col_logits - every_total[:, None])
    col_probs = jnp.exp(col_logits - col_totals[None, :])
    logit_grad = (
        logit_scale * (row_probs + col_probs - 2.0 * identity_part) / (2.0 * pair_total)
    ).astype(bfloat)
    unit_grad = jnp.einsum("ij,id->jd", logit_grad, image_all, preferred_element_type=single)
    unused, unit_back = jax.vjp(unit_rows, text_pooled)
    pooled_grad = unit_back(unit_grad)[0]
    upstream = jnp.einsum("tj,jd->td", pooling, pooled_grad, precision=lax.Precision.HIGHEST)
    input_grad, attn_grad, mlp_grad, vector_grad = block_backward(
        upstream, saved_state, attn_weight, mlp_weight, vectors, allowed
    )
    attn_sum, mlp_sum, vector_sum = (
        lax.psum_scatter(attn_grad, "dp", scatter_dimension=0, tiled=True),
        lax.psum_scatter(mlp_grad, "dp", scatter_dimension=1, tiled=True),
        lax.psum_scatter(vector_grad, "dp", scatter_dimension=1, tiled=True),
    )
    squares = sum_squares((attn_sum, mlp_sum, vector_sum))
    square_total = lax.psum(squares, "dp")
    grad_norm = jnp.sqrt(square_total)
    factor = jnp.minimum(1.0, clip_norm / (grad_norm + 1e-06))
    attn_state = adam_update(
        attn_master, attn_sum, attn_first, attn_second, factor, learn_rate, weight_decay
    )
    mlp_state = adam_update(
        mlp_master, mlp_sum, mlp_first, mlp_second, factor, learn_rate, weight_decay
    )
    vector_state = adam_update(
        vector_master, vector_sum, vector_first, vector_second, factor, vector_rate, 0.0
    )
    return (
        input_grad,
        grad_norm,
        attn_sum,
        mlp_sum,
        vector_sum,
        attn_state[0],
        mlp_state[0],
        vector_state[0],
        attn_state[1],
        mlp_state[1],
        vector_state[1],
        attn_state[2],
        mlp_state[2],
        vector_state[2],
    )


def solution(mesh):
    in_specs = (
        P("dp", None),
        P("dp", None),
        P("dp", None),
        P(),
        P(),
        P(),
        P("dp", None),
        P(None, "dp", None),
        P(None, "dp"),
        P("dp", None),
        P(None, "dp", None),
        P(None, "dp"),
        P("dp", None),
        P(None, "dp", None),
        P(None, "dp"),
    )
    out_specs = (
        P("dp", None),
        P(),
        P("dp", None),
        P(None, "dp", None),
        P(None, "dp"),
        P("dp", None),
        P(None, "dp", None),
        P(None, "dp"),
        P("dp", None),
        P(None, "dp", None),
        P(None, "dp"),
        P("dp", None),
        P(None, "dp", None),
        P(None, "dp"),
    )
    return jax.shard_map(shards, mesh=mesh, in_specs=in_specs, out_specs=out_specs, check_vma=False)
```

profile of v0, /device:TPU:1, one launch (start us, length us, event | category | flops | bytes accessed | tf_op | source)
XLA Modules:
  0.0 1147.1 jit_solution(17260733578758206693)
XLA Ops:
  11.3 38.7 %all-gather = bf16[128,6,12]{2,1,0:T(8,128)(2,1)S(1)} all-gather(bf16[1,6,12]{2,1,0:T(8,128)(2,1)S(1)} %convert_bitcast_fusion.2), channel_id=1, replica_groups=mesh['dp'=128] {'dp'}, dimensions={0}, use_global_device_ids=true | all-gather | bytes 18576 | tf_op jit(solution)/shard_map/all_gather | solution.py:210
  52.1 9.3 fusion.11
  61.4 17.7 %reshape.254 = bf16[24,50,3,12,64]{4,3,2,1,0:T(8,128)(2,1)} reshape(bf16[1200,2304]{1,0:T(8,128)(2,1)} %fusion.11) | data formatting | bytes 11059200 | tf_op jit(solution)/shard_map/reshape | solution.py:66
  79.1 10.9 fusion.170
  90.0 4.7 fusion.44
  94.7 14.0 %fusion.176 = (f32[24,12,50]{2,1,0:T(8,128)}, f32[24,12,50,50]{2,3,1,0:T(8,128)S(1)}) fusion(f32[24,12,50,50]{2,3,1,0:T(8,128)S(1)} %fusion.44), kind=kOutput, calls=%fused_computation.263 | output fusion | flops 2880049 | bytes 5817600 | tf_op jit(solution)/shard_map/sub | solution.py:69
  108.7 6.8 convert_bitcast_fusion
  115.5 6.8 copy.158
  122.3 7.1 convert_element_type.141
  129.5 3.8 fusion.177
  135.7 21.1 %fusion.38 = f32[1200,768]{1,0:T(8,128)} fusion(f32[1200,768]{1,0:T(8,128)} %copy-done.9, bf16[2,768,3072]{2,1,0:T(8,128)(2,1)} %param.19, f32[3072]{0:T(1024)S(1)} %add.332, f32[768]{0:T(1024)S(1)} %get-tuple-element.98, f32[768]{0:T(1024)S(1)} %get-tuple-element.92, f32[768]{0:T(1024)S(1)} %get-tuple-element.91, f32[1200]{0:T(1024)S(1)} %add_rsqrt_fusion, ...), kind=kOutput, calls=%fused_computation.50 | convolution fusion | flops 11367936000 | bytes 20527488 | tf_op jit(solution)/shard_map/tf,df->td/dot_general | solution.py:89
  156.7 4.9 reshape.237
  167.1 7.8 reshape.250
  174.9 3.7 fusion.32
  178.6 4.6 reshape.238
  183.2 5.2 fusion.172
  202.5 19.7 %fusion.171 = (bf16[1,768,3072]{2,0,1:T(2,128)(2,1)S(1)}, bf16[1,768,3072]{2,0,1:T(2,128)(2,1)}) fusion(bf16[2,768,3072]{2,0,1:T(2,128)(2,1)} %all-gather.9.cloned.1.call-done), kind=kLoop, calls=%fused_computation.258 | loop fusion | bytes 18874368 | tf_op jit(solution)/shard_map/slice | solution.py:83
  225.9 8.6 fusion.98
  236.2 3.8 fusion.178
  240.3 61.7 %all-gather.11.cloned.1.call-done = bf16[3072,768]{1,0:T(8,128)(2,1)} async-done(((bf16[24,768]{1,0:T(8,128)(2,1)}), bf16[3072,768]{1,0:T(8,128)(2,1)}) %all-gather.11.cloned.1.call-update) | async-done | bytes 4718608 | tf_op jit(solution)/shard_map/all_gather | solution.py:233
  301.9 3.8 fusion.179
  306.1 62.7 %all-reduce = f32[3072]{0:T(1024)S(1)} all-reduce(f32[3072]{0:T(1024)S(1)} %add_dynamic-update-slice_fusion), channel_id=1, replica_groups=mesh['dp'=128] {'dp'}, use_global_device_ids=true, to_apply=%add | all-reduce | flops 3072 | bytes 24576
  373.3 9.4 convert_reduce_fusion.2
  388.1 5.6 convolution_bitcast_fusion
  395.1 5.0 pad_maximum_fusion
  400.1 37.0 %copy.174 = f32[2,768,3072]{2,0,1:T(2,128)} copy(f32[2,768,3072]{2,1,0:T(8,128)S(1)} %pad_maximum_fusion) | data formatting | bytes 37748736 | tf_op jit(solution)/shard_map/stack | solution.py:157
  445.1 4.0 fusion.105
  449.1 6.8 fusion.87
  455.9 7.0 fusion.90
  467.6 4.6 copy.172
  472.2 6.8 convert_element_type.167
  479.0 3.7 fusion.180
  482.7 5.1 fusion.160
  487.7 9.0 pad_maximum_fusion.1
  496.8 365.3 %fusion = f32[8,3072]{1,0:T(8,128)S(1)} fusion(f32[768,3072]{1,0:T(8,128)} %pad_maximum_fusion.1), kind=kCustom, calls=%all-reduce-scatter | all-reduce-scatter fusion | flops 3145729 | bytes 9535488
  865.4 4.2 fusion.164
  877.5 4.2 collective-permute-start.15
  885.1 16.4 %collective-permute-start.17 = (f32[8,3072]{1,0:T(8,128)S(1)}, f32[8,3072]{1,0:T(8,128)S(1)}, u32[]{:S(2)}, u32[]{:S(2)}) collective-permute-start(f32[8,3072]{1,0:T(8,128)S(1)} %fusion), channel_id=1, source_target_pairs={{0,18},{1,19},{2,20},{3,21},{4,22},{5,23},{6,24},{7,25},{8,26},{9,... | collective-permute-start | bytes 294920
  901.5 5.5 collective-permute-start.18
  907.7 3.4 collective-permute-start.19
  928.0 4.3 collective-permute-start.27
  933.8 4.8 collective-permute-start.28
  945.4 64.1 %all-reduce.3 = f32[12,768]{1,0:T(8,128)S(1)} all-reduce(f32[12,768]{1,0:T(8,128)S(1)} %concatenate.15), channel_id=4, replica_groups=mesh['dp'=128] {'dp'}, use_global_device_ids=true, to_apply=%region_39.40.clone | all-reduce | flops 9216 | bytes 73728
  1009.5 3.5 collective-permute-start.5
  1015.6 3.6 collective-permute-start.7
  1022.2 3.5 collective-permute-start.9
  1027.7 33.3 %concatenate.16 = f32[262,3072]{1,0:T(8,128)S(1)} concatenate(f32[6,3072]{1,0:T(8,128)} %copy-done.20, f32[8,3072]{1,0:T(8,128)} %copy-done.44, f32[8,3072]{1,0:T(8,128)} %copy-done.42, f32[8,3072]{1,0:T(8,128)} %copy-done.41, f32[8,3072]{1,0:T(8,128)} %copy-done.40, f32[8,3072]{1,0:T(8,128)} %copy-done.39, f32[8,3072]{1,0:T(8,128)} %copy-done.38, f32[8,3072]{1,0:T(8,128)} %copy-done.37, ...), dimensions={0} | concatenate | bytes 6438912
  1065.4 68.5 %psum.7 = f32[]{:T(128)} all-reduce(f32[]{:T(128)S(6)} %add.376), channel_id=1, replica_groups=mesh['dp'=128] {'dp'}, use_global_device_ids=true, to_apply=%region_41.42 | all-reduce | flops 1 | bytes 8 | tf_op jit(solution)/shard_map/psum | solution.py:268
  (290 shorter events, 112.0 us)
Async XLA Ops:
  7.2 159.9 %all-gather.13.cloned.1.call-start = ((), (), s32[]{:S(2)}) async-start(), calls=%async_computation.3 | async-start | bytes 6340608 | tf_op jit(solution)/shard_map/all_gather | solution.py:208
  8.9 193.6 %all-gather.9.cloned.1.call-start = ((), (), s32[]{:S(2)}) async-start(), calls=%async_computation.1 | async-start | bytes 9510912 | tf_op jit(solution)/shard_map/all_gather | solution.py:209
  10.6 225.6 %all-gather.7.cloned.1.call-start = ((), (), s32[]{:S(2)}) async-start(), calls=%async_computation | async-start | bytes 4755456 | tf_op jit(solution)/shard_map/all_gather | solution.py:232
  165.1 136.8 %all-gather.11.cloned.1.call-start = ((), (), s32[]{:S(2)}) async-start(), calls=%async_computation.2 | async-start | bytes 4755456 | tf_op jit(solution)/shard_map/all_gather | solution.py:233
  236.1 825.6 %all-reduce.7.cloned.1.call-start = ((), (), s32[]{:S(2)}) async-start(), calls=%async_computation.4 | async-start | bytes 37748736
  236.2 65.8 %copy-start.17 = (bf16[24,768]{1,0:T(8,128)(2,1)S(1)}, bf16[24,768]{1,0:T(8,128)(2,1)}, u32[]{:S(2)}) copy-start(bf16[24,768]{1,0:T(8,128)(2,1)} %multiply_convert_fusion.5) | copy-start | bytes 110596
  862.1 12.7 %collective-permute-start = (f32[8,3072]{1,0:T(8,128)S(1)}, f32[8,3072]{1,0:T(8,128)S(1)}, u32[]{:S(2)}, u32[]{:S(2)}) collective-permute-start(f32[8,3072]{1,0:T(8,128)S(1)} %fusion), channel_id=1, source_target_pairs={{0,1},{1,2},{2,3},{3,4},{4,5},{5,6},{6,7},{7,8},{8,9},{9,10},{10,1... | collective-permute-start | bytes 294920
  864.1 9.5 collective-permute-start.31
  869.6 6.6 collective-permute-start.1
  870.9 6.6 collective-permute-start.10
  872.2 9.6 collective-permute-start.11
  873.5 60.3 %copy-start.20 = (f32[6,3072]{1,0:T(8,128)}, f32[6,3072]{1,0:T(8,128)S(1)}, u32[]{:S(2)}) copy-start(f32[6,3072]{1,0:T(8,128)S(1)} %collective-permute-done.31) | copy-start | bytes 221188
  873.5 11.5 %collective-permute-start.12 = (f32[8,3072]{1,0:T(8,128)S(1)}, f32[8,3072]{1,0:T(8,128)S(1)}, u32[]{:S(2)}, u32[]{:S(2)}) collective-permute-start(f32[8,3072]{1,0:T(8,128)S(1)} %fusion), channel_id=1, source_target_pairs={{0,13},{1,14},{2,15},{3,16},{4,17},{5,18},{6,19},{7,20},{8,21},{9,... | collective-permute-start | bytes 294920
  874.9 59.0 %copy-start.19 = (f32[8,3072]{1,0:T(8,128)}, f32[8,3072]{1,0:T(8,128)S(1)}, u32[]{:S(2)}) copy-start(f32[8,3072]{1,0:T(8,128)S(1)} %collective-permute-done) | copy-start | bytes 294916
  874.9 26.6 %collective-permute-start.13 = (f32[8,3072]{1,0:T(8,128)S(1)}, f32[8,3072]{1,0:T(8,128)S(1)}, u32[]{:S(2)}, u32[]{:S(2)}) collective-permute-start(f32[8,3072]{1,0:T(8,128)S(1)} %fusion), channel_id=1, source_target_pairs={{0,14},{1,15},{2,16},{3,17},{4,18},{5,19},{6,20},{7,21},{8,22},{9,... | collective-permute-start | bytes 294920
  876.2 31.5 %collective-permute-start.14 = (f32[8,3072]{1,0:T(8,128)S(1)}, f32[8,3072]{1,0:T(8,128)S(1)}, u32[]{:S(2)}, u32[]{:S(2)}) collective-permute-start(f32[8,3072]{1,0:T(8,128)S(1)} %fusion), channel_id=1, source_target_pairs={{0,15},{1,16},{2,17},{3,18},{4,19},{5,20},{6,21},{7,22},{8,23},{9,... | collective-permute-start | bytes 294920
  877.5 33.6 %collective-permute-start.15 = (f32[8,3072]{1,0:T(8,128)S(1)}, f32[8,3072]{1,0:T(8,128)S(1)}, u32[]{:S(2)}, u32[]{:S(2)}) collective-permute-start(f32[8,3072]{1,0:T(8,128)S(1)} %fusion), channel_id=1, source_target_pairs={{0,16},{1,17},{2,18},{3,19},{4,20},{5,21},{6,22},{7,23},{8,24},{9,... | collective-permute-start | bytes 294920
  881.8 32.4 %collective-permute-start.16 = (f32[8,3072]{1,0:T(8,128)S(1)}, f32[8,3072]{1,0:T(8,128)S(1)}, u32[]{:S(2)}, u32[]{:S(2)}) collective-permute-start(f32[8,3072]{1,0:T(8,128)S(1)} %fusion), channel_id=1, source_target_pairs={{0,17},{1,18},{2,19},{3,20},{4,21},{5,22},{6,23},{7,24},{8,25},{9,... | collective-permute-start | bytes 294920
  885.0 48.8 %copy-start.24 = (f32[8,3072]{1,0:T(8,128)}, f32[8,3072]{1,0:T(8,128)S(1)}, u32[]{:S(2)}) copy-start(f32[8,3072]{1,0:T(8,128)S(1)} %collective-permute-done.12) | copy-start | bytes 294916
  885.1 31.2 %collective-permute-start.17 = (f32[8,3072]{1,0:T(8,128)S(1)}, f32[8,3072]{1,0:T(8,128)S(1)}, u32[]{:S(2)}, u32[]{:S(2)}) collective-permute-start(f32[8,3072]{1,0:T(8,128)S(1)} %fusion), channel_id=1, source_target_pairs={{0,18},{1,19},{2,20},{3,21},{4,22},{5,23},{6,24},{7,25},{8,26},{9,... | collective-permute-start | bytes 294920
  901.5 16.7 %collective-permute-start.18 = (f32[8,3072]{1,0:T(8,128)S(1)}, f32[8,3072]{1,0:T(8,128)S(1)}, u32[]{:S(2)}, u32[]{:S(2)}) collective-permute-start(f32[8,3072]{1,0:T(8,128)S(1)} %fusion), channel_id=1, source_target_pairs={{0,19},{1,20},{2,21},{3,22},{4,23},{5,24},{6,25},{7,26},{8,27},{9,... | collective-permute-start | bytes 294920
  907.7 11.9 %collective-permute-start.19 = (f32[8,3072]{1,0:T(8,128)S(1)}, f32[8,3072]{1,0:T(8,128)S(1)}, u32[]{:S(2)}, u32[]{:S(2)}) collective-permute-start(f32[8,3072]{1,0:T(8,128)S(1)} %fusion), channel_id=1, source_target_pairs={{0,20},{1,21},{2,22},{3,23},{4,24},{5,25},{6,26},{7,27},{8,28},{9,... | collective-permute-start | bytes 294920
  911.1 10.4 collective-permute-start.2
  914.2 9.8 collective-permute-start.20
  916.2 9.1 collective-permute-start.21
  918.2 9.0 collective-permute-start.22
  919.6 14.2 %collective-permute-start.23 = (f32[8,3072]{1,0:T(8,128)S(1)}, f32[8,3072]{1,0:T(8,128)S(1)}, u32[]{:S(2)}, u32[]{:S(2)}) collective-permute-start(f32[8,3072]{1,0:T(8,128)S(1)} %fusion), channel_id=1, source_target_pairs={{0,24},{1,25},{2,26},{3,27},{4,28},{5,29},{6,30},{7,31},{8,32},{9,... | collective-permute-start | bytes 294920
  921.5 17.1 %collective-permute-start.24 = (f32[8,3072]{1,0:T(8,128)S(1)}, f32[8,3072]{1,0:T(8,128)S(1)}, u32[]{:S(2)}, u32[]{:S(2)}) collective-permute-start(f32[8,3072]{1,0:T(8,128)S(1)} %fusion), channel_id=1, source_target_pairs={{0,25},{1,26},{2,27},{3,28},{4,29},{5,30},{6,31},{7,32},{8,33},{9,... | collective-permute-start | bytes 294920
  924.0 17.0 %collective-permute-start.25 = (f32[8,3072]{1,0:T(8,128)S(1)}, f32[8,3072]{1,0:T(8,128)S(1)}, u32[]{:S(2)}, u32[]{:S(2)}) collective-permute-start(f32[8,3072]{1,0:T(8,128)S(1)} %fusion), channel_id=1, source_target_pairs={{0,26},{1,27},{2,28},{3,29},{4,30},{5,31},{6,32},{7,33},{8,34},{9,... | collective-permute-start | bytes 294920
  925.4 17.0 %collective-permute-start.26 = (f32[8,3072]{1,0:T(8,128)S(1)}, f32[8,3072]{1,0:T(8,128)S(1)}, u32[]{:S(2)}, u32[]{:S(2)}) collective-permute-start(f32[8,3072]{1,0:T(8,128)S(1)} %fusion), channel_id=1, source_target_pairs={{0,27},{1,28},{2,29},{3,30},{4,31},{5,32},{6,33},{7,34},{8,35},{9,... | collective-permute-start | bytes 294920
  928.0 15.7 %collective-permute-start.27 = (f32[8,3072]{1,0:T(8,128)S(1)}, f32[8,3072]{1,0:T(8,128)S(1)}, u32[]{:S(2)}, u32[]{:S(2)}) collective-permute-start(f32[8,3072]{1,0:T(8,128)S(1)} %fusion), channel_id=1, source_target_pairs={{0,28},{1,29},{2,30},{3,31},{4,32},{5,33},{6,34},{7,35},{8,36},{9,... | collective-permute-start | bytes 294920
  933.8 75.7 %collective-permute-start.28 = (f32[8,3072]{1,0:T(8,128)S(1)}, f32[8,3072]{1,0:T(8,128)S(1)}, u32[]{:S(2)}, u32[]{:S(2)}) collective-permute-start(f32[8,3072]{1,0:T(8,128)S(1)} %fusion), channel_id=1, source_target_pairs={{0,29},{1,30},{2,31},{3,32},{4,33},{5,34},{6,35},{7,36},{8,37},{9,... | collective-permute-start | bytes 294920
  938.7 74.3 %collective-permute-start.29 = (f32[8,3072]{1,0:T(8,128)S(1)}, f32[8,3072]{1,0:T(8,128)S(1)}, u32[]{:S(2)}, u32[]{:S(2)}) collective-permute-start(f32[8,3072]{1,0:T(8,128)S(1)} %fusion), channel_id=1, source_target_pairs={{0,30},{1,31},{2,32},{3,33},{4,34},{5,35},{6,36},{7,37},{8,38},{9,... | collective-permute-start | bytes 294920
  941.1 74.5 %collective-permute-start.3 = (f32[8,3072]{1,0:T(8,128)S(1)}, f32[8,3072]{1,0:T(8,128)S(1)}, u32[]{:S(2)}, u32[]{:S(2)}) collective-permute-start(f32[8,3072]{1,0:T(8,128)S(1)} %fusion), channel_id=1, source_target_pairs={{0,4},{1,5},{2,6},{3,7},{4,8},{5,9},{6,10},{7,11},{8,12},{9,13},{1... | collective-permute-start | bytes 294920
  942.4 76.8 %collective-permute-start.30 = (f32[8,3072]{1,0:T(8,128)S(1)}, f32[8,3072]{1,0:T(8,128)S(1)}, u32[]{:S(2)}, u32[]{:S(2)}) collective-permute-start(f32[8,3072]{1,0:T(8,128)S(1)} %fusion), channel_id=1, source_target_pairs={{0,31},{1,32},{2,33},{3,34},{4,35},{5,36},{6,37},{7,38},{8,39},{9,... | collective-permute-start | bytes 294920
  943.8 78.4 %collective-permute-start.4 = (f32[8,3072]{1,0:T(8,128)S(1)}, f32[8,3072]{1,0:T(8,128)S(1)}, u32[]{:S(2)}, u32[]{:S(2)}) collective-permute-start(f32[8,3072]{1,0:T(8,128)S(1)} %fusion), channel_id=1, source_target_pairs={{0,5},{1,6},{2,7},{3,8},{4,9},{5,10},{6,11},{7,12},{8,13},{9,14},{... | collective-permute-start | bytes 294920
  1009.5 16.9 %collective-permute-start.5 = (f32[8,3072]{1,0:T(8,128)S(1)}, f32[8,3072]{1,0:T(8,128)S(1)}, u32[]{:S(2)}, u32[]{:S(2)}) collective-permute-start(f32[8,3072]{1,0:T(8,128)S(1)} %fusion), channel_id=1, source_target_pairs={{0,6},{1,7},{2,8},{3,9},{4,10},{5,11},{6,12},{7,13},{8,14},{9,15},... | collective-permute-start | bytes 294920
  1013.0 13.4 %collective-permute-start.6 = (f32[8,3072]{1,0:T(8,128)S(1)}, f32[8,3072]{1,0:T(8,128)S(1)}, u32[]{:S(2)}, u32[]{:S(2)}) collective-permute-start(f32[8,3072]{1,0:T(8,128)S(1)} %fusion), channel_id=1, source_target_pairs={{0,7},{1,8},{2,9},{3,10},{4,11},{5,12},{6,13},{7,14},{8,15},{9,16}... | collective-permute-start | bytes 294920
  1015.6 10.7 collective-permute-start.7
  1019.3 7.2 collective-permute-start.8
  1022.2 5.5 collective-permute-start.9
  1026.3 108.3 %copy-start.52 = (f32[12,6]{0,1:T(8,128)S(1)}, f32[12,6]{0,1:T(8,128)}, u32[]{:S(2)}) copy-start(f32[12,6]{0,1:T(8,128)} %param.23) | copy-start | bytes 868
  1026.3 108.3 %copy-start.54 = (f32[12,6]{0,1:T(8,128)S(1)}, f32[12,6]{0,1:T(8,128)}, u32[]{:S(2)}) copy-start(f32[12,6]{0,1:T(8,128)} %param.29) | copy-start | bytes 868
  1026.3 108.3 %copy-start.55 = (f32[12,6]{0,1:T(8,128)S(1)}, f32[12,6]{0,1:T(8,128)}, u32[]{:S(2)}) copy-start(f32[12,6]{0,1:T(8,128)} %param.26) | copy-start | bytes 868
  1026.3 108.9 %copy-start.14 = (f32[2,6,3072]{2,0,1:T(2,128)S(1)}, f32[2,6,3072]{2,0,1:T(2,128)}, u32[]{:S(2)}) copy-start(f32[2,6,3072]{2,0,1:T(2,128)} %param.22) | copy-start | bytes 442372
  1061.6 77.6 %copy-start.16 = (f32[6,3072]{1,0:T(8,128)}, f32[6,3072]{1,0:T(8,128)S(1)}, u32[]{:S(2)}) copy-start(f32[6,3072]{1,0:T(8,128)S(1)} %get-tuple-element.125) | copy-start | bytes 221188
  1063.3 75.9 %copy-start.15 = (f32[2,6,3072]{2,0,1:T(2,128)}, f32[2,6,3072]{2,0,1:T(2,128)S(1)}, u32[]{:S(2)}) copy-start(f32[2,6,3072]{2,0,1:T(2,128)S(1)} %get-tuple-element.123) | copy-start | bytes 442372
  1065.4 73.8 %copy-start.51 = (f32[12,6]{0,1:T(8,128)}, f32[12,6]{0,1:T(8,128)S(1)}, u32[]{:S(2)}) copy-start(f32[12,6]{0,1:T(8,128)S(1)} %copy.176) | copy-start | bytes 868
  (51 other events, 467.2 us)
Sparse Core Ops, SparseCore 0:
  11.7 71.8 all-gather.12
  87.3 68.5 all-gather.8
  165.2 65.6 all-gather.6
  236.2 65.6 all-gather.10
  437.3 222.9 all-reduce.6
where the time goes:
time: 1150 us
  blocking collectives  599 us (52%)
  local copies, waits for them, and re-layouts  185 us (16%)
  matrix products  136 us (12%)
  starting transfers between devices  91.3 us (8%)
  waiting for transfers between devices  61.9 us (5%)
  other arithmetic  53.3 us (5%)
  between operations  19.4 us (2%)
    unnamed x3, blocking collectives  492 us
    unnamed x33, starting transfers between devices  91.1 us
    psum x1, blocking collectives, shards(): square_total = lax.psum(squares, 'dp')  68.5 us
    all_gather x1, waiting for transfers between devices, shards(): lax.all_gather(text_unit, 'dp', axis=0, tiled=True)  61.7 us
    unnamed x128, local copies, waits for them, and re-layouts  51.7 us
    all_gather x1, blocking collectives, shards(): lax.all_gather(vector_master.astype(bfloat), 'dp', axis=1, tiled=True)  38.7 us
    another operation x1, local copies, waits for them, and re-layouts, block_backward(): mlp_grad = jnp.stack([up_grad, down_grad])  37 us
    dot_general x2, matrix products, block_forward(): jnp.einsum('tf,df->td', active, mlp_weight[1], preferred_element_type=sin...  29.7 us
  transfers between devices with their start and end apart: 37, of which 1 were waited for; matrix products, arithmetic and copies ran while one was open for 57% of the time, Pallas kernels for 0%

commit v1 on v0

--- a/solution.py
+++ b/solution.py
@@ -1,6 +1,8 @@
 import jax
 import jax.numpy as jnp
 from jax import lax
+from jax.experimental import pallas as pl
+from jax.experimental.pallas import tpu as pltpu
 from jax.sharding import PartitionSpec as P
 
 STEP = 10
@@ -187,6 +189,539 @@
     return (first_new, second_new, weight - rate * (ratio + decay_rate * weight))
 
 
+MESH = pl.DeviceIdType.MESH
+LINES = 144
+SHARD = 448
+
+
+def place():
+    me = lax.axis_index("dp")
+    return (me // 32, lax.rem(me // 8, 4), lax.rem(me // 2, 4), lax.rem(me, 2))
+
+
+def device(x, z, y, c):
+    return ((x * 4 + z) * 4 + y) * 2 + c
+
+
+def plus(index, step):
+    return lax.rem(index + step, 4)
+
+
+class Wire:
+    def __init__(self, send_sems, recv_sems):
+        self.send_sems, self.recv_sems, self.copies = (send_sems, recv_sems, [])
+
+    def send(self, source, target, to):
+        slot = len(self.copies)
+        copy = pltpu.make_async_remote_copy(
+            src_ref=source,
+            dst_ref=target,
+            send_sem=self.send_sems.at[slot],
+            recv_sem=self.recv_sems.at[slot],
+            device_id=(to,),
+            device_id_type=MESH,
+        )
+        copy.start()
+        self.copies.append(copy)
+        return copy
+
+    def drain(self):
+        for copy in self.copies:
+            copy.wait_send()
+
+
+def greet(peers):
+    barrier = pltpu.get_barrier_semaphore()
+    for peer in peers:
+        pl.semaphore_signal(barrier, inc=1, device_id=(peer,), device_id_type=MESH)
+    pl.semaphore_wait(barrier, len(peers))
+
+
+class Ring:
+    def __init__(self, wire, peer, view):
+        self.wire, self.peer, self.view = (wire, peer, view)
+        self.ahead = wire.send(view(0, None), view(0, None), peer(1))
+        self.behind = wire.send(view(0, None), view(0, None), peer(3))
+
+    def forward(self):
+        self.ahead.wait_recv()
+        self.low = self.wire.send(self.view(3, 0), self.view(3, 0), self.peer(1))
+        self.behind.wait_recv()
+        self.high = self.wire.send(self.view(1, 1), self.view(1, 1), self.peer(3))
+
+    def finish(self):
+        self.low.wait_recv()
+        self.high.wait_recv()
+
+
+def aligned(start, size):
+    return pl.ds(pl.multiple_of(start, 128), size)
+
+
+def halves(start, size, part):
+    if part is None:
+        return aligned(start, size)
+    low = size // 256 * 128
+    return aligned(start, low) if part == 0 else aligned(start + low, size - low)
+
+
+def gather_kernel(
+    attn_ref, mlp_ref, vector_ref, weight, turned, line, lines, natural, small, send_sems, recv_sems
+):
+    x, z, y, c = place()
+    peers_x = lambda k: device(plus(x, k), z, y, c)
+    peers_z = lambda k: device(x, plus(z, k), y, c)
+    peers_y = lambda k: device(x, z, plus(y, k), c)
+    sibling = device(x, z, y, 1 - c)
+    wire = Wire(send_sems, recv_sems)
+    lines[c, y, 0:16] = vector_ref[...]
+    for m in range(3):
+        for j in range(24):
+            columns = slice(j * 128, (j + 1) * 128)
+            rows = attn_ref[:, columns] if m == 0 else mlp_ref[m - 1, :, columns]
+            line[m, pl.ds(j, 6, stride=24), :] = rows
+        lines[c, y, 16 + m * LINES : 16 + (m + 1) * LINES] = line[m].astype(bfloat)
+    greet([p(k) for p in (peers_x, peers_z, peers_y) for k in (1, 2, 3)] + [sibling])
+    spans = [pl.ds(0, 160), pl.ds(160, 144), pl.ds(304, 144)]
+    first = [
+        [wire.send(lines.at[c, y, span], lines.at[c, y, span], peers_y(k)) for k in (1, 3, 2)]
+        for span in spans
+    ]
+    swaps = []
+    for m in range(3):
+        for copy in first[m]:
+            copy.wait_recv()
+        swaps.append(wire.send(lines.at[c, :, spans[m]], lines.at[c, :, spans[m]], sibling))
+
+    def spread(m):
+        swaps[m].wait_recv()
+        for s in range(8):
+            natural[s * LINES : (s + 1) * LINES] = lines[
+                s % 2, s // 2, 16 + m * LINES : 16 + (m + 1) * LINES
+            ].astype(single)
+
+    half = c * 1536
+    quarter = (c * 4 + y) * 384
+    spread(0)
+    for j in range(12):
+        weight[0, x, z, :, aligned((c * 12 + j) * 128, 128)] = natural[
+            pl.ds(c * 12 + j, 48, stride=24), :
+        ].astype(bfloat)
+    for s in range(8):
+        small[s * 6 : (s + 1) * 6] = lines[s % 2, s // 2, 0:16].astype(single)[0:6]
+    turned[x, z] = small[...].astype(bfloat)
+    attn_x = Ring(wire, peers_x, lambda k, part: weight.at[0, plus(x, k), z, :, halves(half, 1536, part)])
+    turn_x = [wire.send(turned.at[x, z], turned.at[x, z], peers_x(k)) for k in (1, 3, 2)]
+    spread(1)
+    for j in range(12):
+        weight[1, x, z, :, aligned((c * 12 + j) * 128, 128)] = natural[
+            pl.ds(c * 12 + j, 48, stride=24), :
+        ].astype(bfloat)
+    up_z = Ring(wire, peers_z, lambda k, part: weight.at[1, x, plus(z, k), :, halves(half, 1536, part)])
+    spread(2)
+    for j in range(3):
+        place_j = (c * 4 + y) * 3 + j
+        weight[2, x, z, :, aligned(place_j * 128, 128)] = natural[
+            pl.ds(place_j, 48, stride=24), :
+        ].astype(bfloat)
+    down_x = Ring(wire, peers_x, lambda k, part: weight.at[2, plus(x, k), z, :, halves(quarter, 384, part)])
+    attn_x.forward()
+    up_z.forward()
+    attn_x.finish()
+    for copy in turn_x:
+        copy.wait_recv()
+    attn_z = Ring(wire, peers_z, lambda k, part: weight.at[0, :, plus(z, k), :, halves(half, 1536, part)])
+    turn_z = [wire.send(turned.at[:, z], turned.at[:, z], peers_z(k)) for k in (1, 3, 2)]
+    up_z.finish()
+    up_x = Ring(wire, peers_x, lambda k, part: weight.at[1, plus(x, k), :, :, halves(half, 1536, part)])
+    down_x.forward()
+    down_x.finish()
+    down_z = Ring(wire, peers_z, lambda k, part: weight.at[2, :, plus(z, k), :, halves(quarter, 384, part)])
+    across = []
+
+    def cross(view):
+        across.append(wire.send(view, view, sibling))
+
+    cross(attn_z.view(0, None))
+    cross(up_x.view(0, None))
+    attn_z.forward()
+    cross(attn_z.view(3, None))
+    cross(attn_z.view(1, None))
+    up_x.forward()
+    cross(up_x.view(3, None))
+    cross(up_x.view(1, None))
+    down_z.forward()
+    down_z.finish()
+    down_y = Ring(
+        wire, peers_y, lambda k, part: weight.at[2, :, :, :, halves((c * 4 + plus(y, k)) * 384, 384, part)]
+    )
+    cross(down_y.view(0, None))
+    attn_z.finish()
+    cross(attn_z.view(2, None))
+    up_x.finish()
+    cross(up_x.view(2, None))
+    down_y.forward()
+    cross(down_y.view(3, None))
+    cross(down_y.view(1, None))
+    down_y.finish()
+    cross(down_y.view(2, None))
+    for copy in turn_z + across:
+        copy.wait_recv()
+    wire.drain()
+
+
+def gather_weights(attn_master, mlp_master, vector_master):
+    vector_lines = jnp.pad(vector_master.T, ((0, 10), (0, 116))).astype(bfloat)
+    copies = 64
+    weight, turned = pl.pallas_call(
+        gather_kernel,
+        out_shape=(
+            jax.ShapeDtypeStruct((3, 4, 4, 48, 3072), bfloat),
+            jax.ShapeDtypeStruct((4, 4, 48, 128), bfloat),
+        ),
+        in_specs=[pl.BlockSpec(memory_space=pltpu.VMEM)] * 3,
+        out_specs=[pl.BlockSpec(memory_space=pltpu.VMEM)] * 2,
+        scratch_shapes=[
+            pltpu.VMEM((3, LINES, 128), single),
+            pltpu.VMEM((2, 4, SHARD, 128), bfloat),
+            pltpu.VMEM((8 * LINES, 128), single),
+            pltpu.VMEM((48, 128), single),
+            pltpu.SemaphoreType.DMA((copies,)),
+            pltpu.SemaphoreType.DMA((copies,)),
+        ],
+        compiler_params=pltpu.CompilerParams(
+            collective_id=1, has_side_effects=True, vmem_limit_bytes=56 * 2**20
+        ),
+        name="gather_weights",
+    )(attn_master, mlp_master, vector_lines)
+    weight = weight.reshape(3, 768, 3072)
+    return weight[0], weight[1:], turned.reshape(768, 128)[:, :12].T
+
+
+def loss_kernel(
+    image_ref, pooled_ref, grad_ref, images, own, part, near, far, send_sems, recv_sems
+):
+    x, z, y, c = place()
+    peers_x = lambda k: device(plus(x, k), z, y, c)
+    peers_z = lambda k: device(x, plus(z, k), y, c)
+    peers_y = lambda k: device(x, z, plus(y, k), c)
+    sibling = device(x, z, y, 1 - c)
+    wire = Wire(send_sems, recv_sems)
+    group = [(k, d) for k in range(4) for d in range(2) if (k, d) != (0, 0)]
+    plane = [(i, j) for i in range(4) for j in range(4) if (i, j) != (0, 0)]
+    group_peer = lambda k, d: device(x, z, plus(y, k), lax.rem(c + d, 2))
+    plane_peer = lambda i, j: device(plus(x, i), plus(z, j), y, c)
+    own[c] = image_ref[...]
+    greet([group_peer(*g) for g in group] + [plane_peer(*p) for p in plane])
+    swap = wire.send(own.at[c], own.at[c], sibling)
+    swap.wait_recv()
+    lanes = aligned(c * 384, 384)
+    images[x, z, y, :, lanes] = own[:, :, lanes].reshape(48, 384).astype(bfloat)
+    lane = [aligned((c * 3 + o) * 128, 128) for o in range(3)]
+
+    def view_of(o, axes):
+        def view(k, part):
+            index = []
+            for name, here in (("x", x), ("z", z), ("y", y)):
+                if name in axes[:-1]:
+                    index.append(slice(None))
+                elif name == axes[-1]:
+                    index.append(plus(here, k))
+                else:
+                    index.append(here)
+            rows = slice(None) if part is None else (pl.ds(0, 16) if part == 0 else pl.ds(16, 32))
+            return images.at[(*index, rows, lane[o])]
+
+        return view
+
+    orders = ("yzx", "zxy", "xyz")
+    peers = {"x": peers_x, "z": peers_z, "y": peers_y}
+    for step in range(3):
+        rings = [
+            Ring(wire, peers[orders[o][step]], view_of(o, orders[o][: step + 1])) for o in range(3)
+        ]
+        for ring in rings:
+            ring.forward()
+        for ring in rings:
+            ring.finish()
+    mine = images.at[:, :, :, :, aligned(c * 384, 384)]
+    cross = wire.send(mine, mine, sibling)
+    pooled = pooled_ref[...]
+    scale = lax.rsqrt(jnp.sum(pooled * pooled, -1, keepdims=True) + 1e-06)
+    unit = pooled * scale
+    cross.wait_recv()
+    every = images[...].reshape(3072, 768)
+    logits = logit_scale * lax.dot_general(
+        unit.astype(bfloat), every, (((1,), (1,)), ((), ())), preferred_element_type=single
+    )
+    powers = jnp.exp(logits)
+    column = jnp.sum(powers, 1, keepdims=True)
+    rows = jnp.sum(powers, 0, keepdims=True)
+    for k in range(8):
+        part[k : k + 1, :] = rows[:, k * 384 : (k + 1) * 384]
+    near[y, c] = part[...]
+    sent = [wire.send(part, near.at[y, c], group_peer(*g)) for g in group]
+    for copy in sent:
+        copy.wait_recv()
+    total = sum(near[k, d] for k in range(4) for d in range(2))
+    far[x, z] = total
+    sent = [wire.send(far.at[x, z], far.at[x, z], plane_peer(*p)) for p in plane]
+    for copy in sent:
+        copy.wait_recv()
+    total = sum(far[i, j] for i in range(4) for j in range(4))
+    every_row = jnp.concatenate([total[k : k + 1] for k in range(8)], 1)
+    caption = lax.broadcasted_iota(jnp.int32, (24, 3072), 0) + lax.axis_index("dp") * 24
+    image = lax.broadcasted_iota(jnp.int32, (24, 3072), 1)
+    same = (caption == image).astype(single)
+    logit_grad = (
+        logit_scale * (powers / every_row + powers / column - 2.0 * same) / (2.0 * 3072)
+    ).astype(bfloat)
+    unit_grad = jnp.dot(logit_grad, every, preferred_element_type=single)
+    grad_ref[...] = scale * (
+        unit_grad - unit * jnp.sum(unit * unit_grad, -1, keepdims=True)
+    )
+    wire.drain()
+
+
+def pair_gradient(image_unit, text_pooled):
+    copies = 72
+    return pl.pallas_call(
+        loss_kernel,
+        out_shape=jax.ShapeDtypeStruct((24, 768), single),
+        in_specs=[pl.BlockSpec(memory_space=pltpu.VMEM)] * 2,
+        out_specs=pl.BlockSpec(memory_space=pltpu.VMEM),
+        scratch_shapes=[
+            pltpu.VMEM((4, 4, 4, 48, 768), bfloat),
+            pltpu.VMEM((2, 24, 768), single),
+            pltpu.VMEM((8, 384), single),
+            pltpu.VMEM((4, 2, 8, 384), single),
+            pltpu.VMEM((4, 4, 8, 384), single),
+            pltpu.SemaphoreType.DMA((copies,)),
+            pltpu.SemaphoreType.DMA((copies,)),
+        ],
+        compiler_params=pltpu.CompilerParams(
+            collective_id=2, has_side_effects=True, vmem_limit_bytes=56 * 2**20
+        ),
+        name="pair_gradient",
+    )(image_unit, text_pooled)
+
+
+def scatter_kernel(
+    attn_ref,
+    mlp_ref,
+    vector_ref,
+    attn_out,
+    mlp_out,
+    vector_out,
+    square_out,
+    held,
+    from_z,
+    from_x,
+    from_y,
+    total_z,
+    total_x,
+    total_y,
+    late_x,
+    late_z,
+    down_x,
+    down_z,
+    whole,
+    last,
+    flat,
+    third,
+    packed,
+    pieces,
+    landed,
+    sums,
+    vec_c,
+    vec_z,
+    vec_x,
+    vec_y,
+    square,
+    near,
+    far,
+    send_sems,
+    recv_sems,
+):
+    x, z, y, c = place()
+    peers_x = lambda k: device(plus(x, k), z, y, c)
+    peers_z = lambda k: device(x, plus(z, k), y, c)
+    peers_y = lambda k: device(x, z, plus(y, k), c)
+    sibling = device(x, z, y, 1 - c)
+    group = [(k, d) for k in range(4) for d in range(2) if (k, d) != (0, 0)]
+    plane = [(i, j) for i in range(4) for j in range(4) if (i, j) != (0, 0)]
+    group_peer = lambda k, d: device(x, z, plus(y, k), lax.rem(c + d, 2))
+    plane_peer = lambda i, j: device(plus(x, i), plus(z, j), y, c)
+    wire = Wire(send_sems, recv_sems)
+    greet([group_peer(*g) for g in group] + [plane_peer(*p) for p in plane])
+    grads = [attn_ref, mlp_ref.at[0], mlp_ref.at[1]]
+    mine, other = (aligned(c * 1536, 1536), aligned((1 - c) * 1536, 1536))
+    vec_c[c] = vector_ref[...]
+    swap = [wire.send(grads[m].at[:, :, :, other], held.at[m], sibling) for m in range(3)]
+    vec_swap = wire.send(vec_c.at[c], vec_c.at[c], sibling)
+
+    def join(m):
+        swap[m].wait_recv()
+
+        @pl.loop(0, 16)
+        def _(k):
+            i, j = (k // 4, lax.rem(k, 4))
+            held[m, i, j] = held[m, i, j] + grads[m][i, j, :, mine]
+
+    turns = (1, 3, 2)
+    join(0)
+    send_z = [wire.send(held.at[0, :, plus(z, k)], from_z.at[k - 1], peers_z(k)) for k in turns]
+    vec_swap.wait_recv()
+    vec_z[z] = vec_c[0] + vec_c[1]
+    sent_vec_z = [wire.send(vec_z.at[z], vec_z.at[z], peers_z(k)) for k in turns]
+    join(1)
+    send_x = [wire.send(held.at[1, plus(x, k)], from_x.at[k - 1], peers_x(k)) for k in turns]
+    join(2)
+    send_y = [
+        wire.send(held.at[2, :, :, :, aligned(plus(y, k) * 384, 384)], from_y.at[k - 1], peers_y(k))
+        for k in turns
+    ]
+
+    def await_all(copies):
+        for copy in copies:
+            copy.wait_recv()
+
+    await_all(sent_vec_z)
+    vec_x[x] = vec_z[0] + vec_z[1] + vec_z[2] + vec_z[3]
+    sent_vec_x = [wire.send(vec_x.at[x], vec_x.at[x], peers_x(k)) for k in turns]
+    await_all(send_z)
+
+    def add(base, parts):
+        return base.astype(single) + sum(part.astype(single) for part in parts)
+
+    for i in range(4):
+        total_z[i] = add(held[0, i, z], [from_z[k, i] for k in range(3)]).astype(bfloat)
+    late_send_x = [wire.send(total_z.at[plus(x, k)], late_x.at[k - 1], peers_x(k)) for k in turns]
+    await_all(send_x)
+    for i in range(4):
+        total_x[i] = add(held[1, x, i], [from_x[k, i] for k in range(3)]).astype(bfloat)
+    late_send_z = [wire.send(total_x.at[plus(z, k)], late_z.at[k - 1], peers_z(k)) for k in turns]
+    await_all(send_y)
+    quarter = aligned(y * 384, 384)
+    for i in range(4):
+        for j in range(4):
+            total_y[i, j] = add(
+                held[2, i, j, :, quarter], [from_y[k, i, j] for k in range(3)]
+            ).astype(bfloat)
+    down_send_x = [wire.send(total_y.at[plus(x, k)], down_x.at[k - 1], peers_x(k)) for k in turns]
+    await_all(sent_vec_x)
+    vec_y[y] = vec_x[0] + vec_x[1] + vec_x[2] + vec_x[3]
+    sent_vec_y = [wire.send(vec_y.at[y], vec_y.at[y], peers_y(k)) for k in turns]
+    await_all(late_send_x)
+    whole[0] = add(total_z[x], [late_x[k] for k in range(3)])
+    await_all(late_send_z)
+    whole[1] = add(total_x[z], [late_z[k] for k in range(3)])
+    await_all(down_send_x)
+    for j in range(4):
+        last[j] = add(total_y[x, j], [down_x[k, j] for k in range(3)]).astype(bfloat)
+    down_send_z = [wire.send(last.at[plus(z, k)], down_z.at[k - 1], peers_z(k)) for k in turns]
+    for m in range(2):
+        for j in range(12):
+            flat[m, pl.ds(j, 48, stride=12), :] = whole[m, :, j * 128 : (j + 1) * 128]
+    await_all(down_send_z)
+    ended = add(last[z], [down_z[k] for k in range(3)])
+    for j in range(3):
+        third[pl.ds(j, 48, stride=3), :] = ended[:, j * 128 : (j + 1) * 128]
+    packed[160:176] = jnp.zeros((16, 128), single)
+    for s in range(8):
+        packed[0:72] = flat[0, s * 72 : (s + 1) * 72]
+        packed[72:144] = flat[1, s * 72 : (s + 1) * 72]
+        packed[144:162] = third[s * 18 : (s + 1) * 18]
+        pieces[s // 2, s % 2] = packed[...].astype(bfloat)
+    landed[y, c] = pieces[y, c]
+    piece_sent = [
+        wire.send(pieces.at[plus(y, k), lax.rem(c + d, 2)], landed.at[y, c], group_peer(k, d))
+        for k, d in group
+    ]
+    await_all(sent_vec_y)
+    vec_total = vec_y[0] + vec_y[1] + vec_y[2] + vec_y[3]
+    vector_out[...] = vec_total
+    await_all(piece_sent)
+    for h in range(2):
+        for k in range(4):
+            rows = landed[k, h].astype(single)
+            packed[...] = rows if k == 0 else packed[...] + rows
+            sums[...] = rows[144:168]
+            for j in range(3):
+                at = ((h * 4 + k) * 3 + j) * 128
+                mlp_out[1, :, at : at + 128] = sums[pl.ds(j, 6, stride=3), :]
+        for j in range(12):
+            at = (h * 12 + j) * 128
+            attn_out[:, at : at + 128] = packed[pl.ds(j, 6, stride=12), :]
+            mlp_out[0, :, at : at + 128] = packed[pl.ds(72 + j, 6, stride=12), :]
+    lanes = lax.broadcasted_iota(jnp.int32, (16, 768), 1)
+    start = lax.axis_index("dp") * 6
+    owned = jnp.where((lanes >= start) & (lanes < start + 6), vec_total, 0.0)
+    squares = sum_squares((attn_out[...], mlp_out[0], mlp_out[1], owned))
+    square[...] = jnp.broadcast_to(squares, (8, 128))
+    near[y, c] = square[...]
+    sent = [wire.send(square, near.at[y, c], group_peer(*g)) for g in group]
+    await_all(sent)
+    far[x, z] = sum(near[k, d] for k in range(4) for d in range(2))
+    sent = [wire.send(far.at[x, z], far.at[x, z], plane_peer(*p)) for p in plane]
+    await_all(sent)
+    square_out[...] = sum(far[i, j] for i in range(4) for j in range(4))
+    wire.drain()
+
+
+def scatter_gradients(attn_grad, mlp_grad, vector_grad):
+    copies = 72
+    attn = attn_grad.astype(bfloat).reshape(4, 4, 48, 3072)
+    mlp = mlp_grad.astype(bfloat).reshape(2, 4, 4, 48, 3072)
+    vector = jnp.pad(vector_grad, ((0, 4), (0, 0)))
+    vmem = pl.BlockSpec(memory_space=pltpu.VMEM)
+    return pl.pallas_call(
+        scatter_kernel,
+        out_shape=(
+            jax.ShapeDtypeStruct((6, 3072), single),
+            jax.ShapeDtypeStruct((2, 6, 3072), single),
+            jax.ShapeDtypeStruct((16, 768), single),
+            jax.ShapeDtypeStruct((8, 128), single),
+        ),
+        in_specs=[vmem] * 3,
+        out_specs=[vmem] * 4,
+        scratch_shapes=[
+            pltpu.VMEM((3, 4, 4, 48, 1536), bfloat),
+            pltpu.VMEM((3, 4, 48, 1536), bfloat),
+            pltpu.VMEM((3, 4, 48, 1536), bfloat),
+            pltpu.VMEM((3, 4, 4, 48, 384), bfloat),
+            pltpu.VMEM((4, 48, 1536), bfloat),
+            pltpu.VMEM((4, 48, 1536), bfloat),
+            pltpu.VMEM((4, 4, 48, 384), bfloat),
+            pltpu.VMEM((3, 48, 1536), bfloat),
+            pltpu.VMEM((3, 48, 1536), bfloat),
+            pltpu.VMEM((3, 4, 48, 384), bfloat),
+            pltpu.VMEM((3, 48, 384), bfloat),
+            pltpu.VMEM((2, 48, 1536), single),
+            pltpu.VMEM((4, 48, 384), bfloat),
+            pltpu.VMEM((2, 576, 128), single),
+            pltpu.VMEM((144, 128), single),
+            pltpu.VMEM((176, 128), single),
+            pltpu.VMEM((4, 2, 176, 128), bfloat),
+            pltpu.VMEM((4, 2, 176, 128), bfloat),
+            pltpu.VMEM((24, 128), single),
+            pltpu.VMEM((2, 16, 768), single),
+            pltpu.VMEM((4, 16, 768), single),
+            pltpu.VMEM((4, 16, 768), single),
+            pltpu.VMEM((4, 16, 768), single),
+            pltpu.VMEM((8, 128), single),
+            pltpu.VMEM((4, 2, 8, 128), single),
+            pltpu.VMEM((4, 4, 8, 128), single),
+            pltpu.SemaphoreType.DMA((copies,)),
+            pltpu.SemaphoreType.DMA((copies,)),
+        ],
+        compiler_params=pltpu.CompilerParams(
+            collective_id=3, has_side_effects=True, vmem_limit_bytes=56 * 2**20
+        ),
+        name="scatter_gradients",
+    )(attn, mlp, vector)
+
+
 def shards(
     text_input,
     caption_lengths,
@@ -204,11 +739,7 @@
     mlp_second,
     vector_second,
 ):
-    attn_weight, mlp_weight, vector_low = (
-        lax.all_gather(attn_master.astype(bfloat), "dp", axis=0, tiled=True),
-        lax.all_gather(mlp_master.astype(bfloat), "dp", axis=1, tiled=True),
-        lax.all_gather(vector_master.astype(bfloat), "dp", axis=1, tiled=True),
-    )
+    attn_weight, mlp_weight, vector_low = gather_weights(attn_master, mlp_master, vector_master)
     vectors = vector_low.astype(single)
     features = text_input.shape[1]
     row_count, slot_count = caption_lengths.shape
@@ -218,55 +749,24 @@
     full_mask = jnp.ones((pair_count, patches, patches), jnp.bool_)
     image_inputs = image_tokens.astype(single).reshape(pair_count, patches, features)
     image_out, unused = block_forward(image_inputs, image_attn, image_mlp, image_vectors, full_mask)
-    image_unit = unit_rows(jnp.mean(image_out.reshape(pair_count, patches, features), 1)).astype(
-        bfloat
-    )
+    image_unit = unit_rows(jnp.mean(image_out.reshape(pair_count, patches, features), 1))
     slot_ids = caption_slots(caption_lengths, row_len)
     allowed = slot_ids[:, :, None] == slot_ids[:, None, :]
     text_inputs = text_input.astype(single).reshape(row_count, row_len, features)
     text_out, saved_state = block_forward(text_inputs, attn_weight, mlp_weight, vectors, allowed)
     pooling = pool_matrix(caption_lengths, slot_ids)
     text_pooled = jnp.einsum("tj,td->jd", pooling, text_out, precision=lax.Precision.HIGHEST)
-    text_unit = unit_rows(text_pooled).astype(bfloat)
-    image_all, text_all = (
-        lax.all_gather(image_unit, "dp", axis=0, tiled=True),
-        lax.all_gather(text_unit, "dp", axis=0, tiled=True),
-    )
-    pair_total = pair_count * lax.axis_size("dp")
-    offset = lax.axis_index("dp") * pair_count
-    row_logits = logit_scale * jnp.einsum(
-        "id,jd->ij", image_unit, text_all, preferred_element_type=single
-    )
-    row_totals = log_sum_exp(row_logits, 1)
-    col_logits = logit_scale * jnp.einsum(
-        "id,jd->ij", image_all, text_unit, preferred_element_type=single
-    )
-    col_totals = log_sum_exp(col_logits, 0)
-    every_total = lax.all_gather(row_totals, "dp", axis=0, tiled=True)
-    identity_part = (
-        jnp.arange(pair_total, dtype=jnp.int32)[:, None]
-        == offset + jnp.arange(pair_count, dtype=jnp.int32)[None, :]
-    ).astype(single)
-    row_probs = jnp.exp(col_logits - every_total[:, None])
-    col_probs = jnp.exp(col_logits - col_totals[None, :])
-    logit_grad = (
-        logit_scale * (row_probs + col_probs - 2.0 * identity_part) / (2.0 * pair_total)
-    ).astype(bfloat)
-    unit_grad = jnp.einsum("ij,id->jd", logit_grad, image_all, preferred_element_type=single)
-    unused, unit_back = jax.vjp(unit_rows, text_pooled)
-    pooled_grad = unit_back(unit_grad)[0]
+    pooled_grad = pair_gradient(image_unit, text_pooled)
     upstream = jnp.einsum("tj,jd->td", pooling, pooled_grad, precision=lax.Precision.HIGHEST)
     input_grad, attn_grad, mlp_grad, vector_grad = block_backward(
         upstream, saved_state, attn_weight, mlp_weight, vectors, allowed
     )
-    attn_sum, mlp_sum, vector_sum = (
-        lax.psum_scatter(attn_grad, "dp", scatter_dimension=0, tiled=True),
-        lax.psum_scatter(mlp_grad, "dp", scatter_dimension=1, tiled=True),
-        lax.psum_scatter(vector_grad, "dp", scatter_dimension=1, tiled=True),
-    )
-    squares = sum_squares((attn_sum, mlp_sum, vector_sum))
-    square_total = lax.psum(squares, "dp")
-    grad_norm = jnp.sqrt(square_total)
+    attn_sum, mlp_sum, vector_all, square_total = scatter_gradients(
+        attn_grad, mlp_grad, vector_grad
+    )
+    start = lax.axis_index("dp") * 6
+    vector_sum = lax.dynamic_slice_in_dim(vector_all[:12], start, 6, 1)
+    grad_norm = jnp.sqrt(square_total[0, 0])
     factor = jnp.minimum(1.0, clip_norm / (grad_norm + 1e-06))
     attn_state = adam_update(
         attn_master, attn_sum, attn_first, attn_second, factor, learn_rate, weight_decay

time: 1150 us -> 506 us (0.44)
  blocking collectives: 599 us -> 0 us
  Pallas kernels: 0 us -> 213 us
  starting transfers between devices: 91.3 us -> 0 us
  local copies, waits for them, and re-layouts: 185 us -> 115 us
  waiting for transfers between devices: 61.9 us -> 0 us
  matrix products: 136 us -> 119 us
  between operations: 19.4 us -> 3.69 us
    unnamed x3 -> x0, blocking collectives: 492 us -> none
    pallas_call x0 -> x3, Pallas kernels: none -> 213 us  [the longest x1 83.2 us: scatter_gradients(): pl.pallas_call(scatter_kernel, out_shape=(jax.ShapeDtypeStruct((6, 3072),...]
    unnamed x33 -> x0, starting transfers between devices: 91.1 us -> none
    psum x1 -> x0, blocking collectives: 68.5 us -> none  [shards(): square_total = lax.psum(squares, 'dp')]
    all_gather x4 -> x0, waiting for transfers between devices: 61.7 us -> none  [the longest x1 61.7 us: shards(): lax.all_gather(text_unit, 'dp', axis=0, tiled=True)]
    all_gather x1 -> x0, blocking collectives: 38.7 us -> none  [shards(): lax.all_gather(vector_master.astype(bfloat), 'dp', axis=1, tiled=True)]
    another operation x2 -> x1, local copies, waits for them, and re-layouts: 37 us -> 0.01 us  [the longest x1 37 us: block_backward(): mlp_grad = jnp.stack([up_grad, down_grad])]
    unnamed x128 -> x153, local copies, waits for them, and re-layouts: 51.7 us -> 18.3 us
  transfers between devices with their start and end apart: 37 -> 0, of which waited for: 1 -> 0; matrix products, arithmetic and copies ran while one was open for 57% -> 0% of each run, Pallas kernels for 0% -> 0%
where the time goes in v1:
time: 506 us; the launch traced here: 501 us
  Pallas kernels  213 us (42%)
  matrix products  119 us (24%)
  local copies, waits for them, and re-layouts  115 us (23%)
  other arithmetic  49.7 us (10%)
    pallas_call x1, Pallas kernels, scatter_gradients(): pl.pallas_call(scatter_kernel, out_shape=(jax.ShapeDtypeStruct((6, 3072),...  83.2 us
    pallas_call x1, Pallas kernels, gather_weights(): pl.pallas_call(gather_kernel, out_shape=(jax.ShapeDtypeStruct((3, 4, 4, 4...  79.9 us
    pallas_call x1, Pallas kernels, pair_gradient(): pl.pallas_call(loss_kernel, out_shape=jax.ShapeDtypeStruct((24, 768), sin...  50 us
    dot_general x2, matrix products, block_forward(): jnp.einsum('tf,df->td', active, mlp_weight[1], preferred_element_type=sin...  23.8 us
    reshape x2, local copies, waits for them, and re-layouts, block_forward(): triple.astype(bfloat).reshape(sequences, length, 3, head_count, 64)  22.3 us
    unnamed x153, local copies, waits for them, and re-layouts  18.3 us
    convert_element_type x3, local copies, waits for them, and re-layouts, block_backward(): jnp.stack([query_grad, key_grad, value_grad], 2).astype(bfloat)  18 us
    convert_element_type x4, local copies, waits for them, and re-layouts, block_forward(): attended = attended.reshape(sequences * length, features).astype(bfloat)  17.6 us

profile of v1, /device:TPU:1, one launch (start us, length us, event | category | flops | bytes accessed | tf_op | source)
XLA Modules:
  0.0 501.1 jit_solution(3127806628408389663)
XLA Ops:
  0.7 1.8 copy.183.mlp_ref
  3.7 79.9 %gather_weights.1 = (bf16[3,4,4,48,3072]{4,3,2,1,0:T(8,128)(2,1)}, bf16[4,4,48,128]{3,2,1,0:T(8,128)(2,1)}) custom-call(f32[6,3072]{1,0:T(8,128)} %attn_ref.1, f32[2,6,3072]{2,1,0:T(8,128)} %copy.183.mlp_ref, bf16[16,128]{1,0:T(8,128)(2,1)} %pad.9.vector_ref), custom_call_target="tpu_custom_call" | custom-call | tf_op jit(solution)/shard_map/gather_weights/pallas_call | solution.py:376
  87.1 1.8 convert_reduce_fusion.1
  89.6 9.2 %fusion.10 = bf16[1200,2304]{1,0:T(8,128)(2,1)} fusion(f32[2304]{0:T(1024)S(1)} %get-tuple-element.149, bf16[768,3072]{1,0:T(8,128)(2,1)} %param.18, bf16[1200,768]{1,0:T(8,128)(2,1)S(1)} %copy-done.3, f32[768]{0:T(1024)S(1)} %get-tuple-element.165, f32[768]{0:T(1024)S(1)} %get-tuple-element.164, f32[1200]{0:T(1024)S(1)} %add_rsqrt_fusion.1, ...), kind=kOutput, calls=%fused_computation.12 | convolution fusion | flops 4257792000 | bytes 10936704 | tf_op jit(solution)/shard_map/dot_general | solution.py:67
  98.9 17.6 %reshape.251 = bf16[24,50,3,12,64]{4,3,2,1,0:T(8,128)(2,1)} reshape(bf16[1200,2304]{1,0:T(8,128)(2,1)} %fusion.10) | data formatting | bytes 11059200 | tf_op jit(solution)/shard_map/reshape | solution.py:68
  116.4 10.9 %fusion.157 = (bf16[24,50,1,12,64]{4,3,2,1,0:T(8,128)(2,1)}, bf16[24,50,1,12,64]{4,3,2,1,0:T(8,128)(2,1)S(1)}, bf16[24,50,1,12,64]{4,3,2,1,0:T(8,128)(2,1)}) fusion(bf16[24,50,3,12,64]{4,3,2,1,0:T(8,128)(2,1)} %reshape.251), kind=kLoop, calls=%fused_computation.225 | loop fusion | bytes 11059200 | tf_op jit(solution)/shard_map/slice | solution.py:76
  127.3 4.7 fusion.43
  132.0 14.0 %fusion.161 = (f32[24,12,50]{2,1,0:T(8,128)}, f32[24,12,50,50]{2,3,1,0:T(8,128)S(1)}) fusion(f32[24,12,50,50]{2,3,1,0:T(8,128)S(1)} %fusion.43), kind=kOutput, calls=%fused_computation.229 | output fusion | flops 2880049 | bytes 5817600 | tf_op jit(solution)/shard_map/sub | solution.py:71
  146.0 6.8 %convert_bitcast_fusion = bf16[24,50,12,64]{3,1,2,0:T(8,128)(2,1)} fusion(f32[24,12,50,50]{2,3,1,0:T(8,128)S(1)} %get-tuple-element.152, f32[24,12,50]{2,1,0:T(8,128)} %get-tuple-element.151, bf16[24,50,1,12,64]{4,3,2,1,0:T(8,128)(2,1)} %get-tuple-element.135), kind=kOutput, calls=%fused_computation.55 | convolution fusion | flops 94521600 | bytes 6624000 | tf_op jit(solution)/shard_map/nhqk,nkhd->nqhd/dot_general | solution.py:75
  152.8 6.8 %copy.182 = bf16[24,50,12,64]{1,0,3,2:T(8,128)(2,1)} copy(bf16[24,50,12,64]{3,1,2,0:T(8,128)(2,1)} %convert_bitcast_fusion) | data formatting | bytes 3686400 | tf_op jit(solution)/shard_map/convert_element_type | solution.py:78
  159.6 7.1 %convert_element_type.139 = bf16[1200,768]{0,1:T(8,128)(2,1)} reshape(bf16[24,50,12,64]{1,0,3,2:T(8,128)(2,1)} %copy.182) | data formatting | bytes 3686400 | tf_op jit(solution)/shard_map/convert_element_type | solution.py:78
  166.8 5.4 %fusion.162 = (f32[1200]{0:T(1024)S(1)}, f32[1200,768]{1,0:T(8,128)}) fusion(f32[768]{0:T(1024)S(1)} %copy-done.56, bf16[1200,768]{0,1:T(8,128)(2,1)} %convert_element_type.139, bf16[768,3072]{1,0:T(8,128)(2,1)} %param.18, bf16[1200,768]{1,0:T(8,128)(2,1)S(1)} %copy-done.4), kind=kOutput, calls=%fused_computation.230 | convolution fusion | flops 1419262848 | bytes 8683200 | tf_op jit(solution)/shard_map/dot_general | solution.py:81
  172.2 2.6 multiply_reduce_fusion.1
  174.8 20.9 %fusion.37 = f32[1200,768]{1,0:T(8,128)} fusion(f32[1200,768]{1,0:T(8,128)} %get-tuple-element.154, bf16[2,768,3072]{2,1,0:T(8,128)(2,1)} %param.19, f32[3072]{0:T(1024)S(1)} %add.290, f32[768]{0:T(1024)S(1)} %get-tuple-element.163, f32[768]{0:T(1024)S(1)} %get-tuple-element.169, f32[768]{0:T(1024)S(1)} %copy-done.55, f32[1200]{0:T(1024)S(1)} %add_rsqrt_fusion, ...), kind=kOutput, calls=%fused_computation.49 | convolution fusion | flops 11367936000 | bytes 20527488 | tf_op jit(solution)/shard_map/tf,df->td/dot_general | solution.py:91
  195.7 4.9 reshape.239
  200.6 2.6 reduce_sum.238
  204.0 9.9 %fusion.158 = (bf16[1,4,4,48,3072]{4,3,2,1,0:T(8,128)(2,1)}, bf16[1,4,4,48,3072]{4,3,2,1,0:T(8,128)(2,1)}, bf16[1,4,4,48,3072]{4,3,2,1,0:T(8,128)(2,1)S(1)}) fusion(bf16[3,4,4,48,3072]{4,3,2,1,0:T(8,128)(2,1)} %get-tuple-element.21), kind=kLoop, calls=%fused_computation.226 | loop fusion | bytes 28311552 | tf_op jit(solution)/shard_map/slice | solution.py:85
  217.8 4.7 reshape.241
  222.5 5.3 %fusion.159 = (bf16[6,64,1,12,64]{4,3,2,1,0:T(8,128)(2,1)S(1)}, bf16[6,64,1,12,64]{4,3,2,1,0:T(8,128)(2,1)}, bf16[6,64,1,12,64]{4,3,2,1,0:T(8,128)(2,1)}) fusion(bf16[6,64,3,12,64]{4,3,2,1,0:T(8,128)(2,1)} %reshape.241), kind=kLoop, calls=%fused_computation.227 | loop fusion | bytes 3538944 | tf_op jit(solution)/shard_map/slice | solution.py:76
  227.7 1.9 copy.226
  230.0 2.7 fusion.163
  236.5 2.3 copy.189
  240.2 2.2 fusion.164
  243.9 4.6 convolution_add_fusion.2
  248.6 3.0 fusion.94
  253.3 50.0 %pair_gradient.1 = f32[24,768]{1,0:T(8,128)} custom-call(f32[24,768]{1,0:T(8,128)} %broadcast_multiply_fusion.image_ref, f32[24,768]{1,0:T(8,128)} %fusion.122.pooled_ref), custom_call_target="tpu_custom_call" | custom-call | tf_op jit(solution)/shard_map/pair_gradient/pallas_call | solution.py:488
  303.4 2.2 fusion.121
  306.2 8.9 %convert_reduce_fusion.2 = (f32[3072]{0:T(1024)}, bf16[384,3072]{1,0:T(8,128)(2,1)S(1)}) fusion(f32[384,3072]{1,0:T(8,128)} %copy-done.62, bf16[768,3072]{1,0:T(8,128)(2,1)} %bitcast.112, f32[384,768]{1,0:T(8,128)S(1)} %fusion.121), kind=kOutput, calls=%fused_computation.39 | convolution fusion | flops 1838183424 | bytes 12988416 | tf_op jit(solution)/shard_map/dot_general | solution.py:117
  315.2 2.8 multiply_reduce_fusion.3
  321.4 1.9 convolution_convert_fusion.5
  323.3 1.9 reshape.242
  325.2 3.9 convolution_bitcast_fusion
  329.2 2.2 fusion.101
  331.4 6.7 %fusion.87 = bf16[6,64,1,12,64]{4,1,3,0,2:T(8,128)(2,1)} fusion(f32[6,12,64,64]{2,3,1,0:T(8,128)} %fusion.101, f32[6,12,64,64]{2,3,1,0:T(8,128)} %copy-done.2, f32[6,12,64]{2,1,0:T(8,128)S(1)} %copy-done.15, bf16[6,64,1,12,64]{4,3,2,1,0:T(8,128)(2,1)} %get-tuple-element.143), kind=kOutput, calls=%fused_computation.99 | convolution fusion | flops 39817792 | bytes 3557376 | tf_op jit(solution)/shard_map/nhqk,nqhd->nkhd/dot_general | solution.py:146
  338.1 6.6 %fusion.84 = bf16[6,64,1,12,64]{4,1,3,0,2:T(8,128)(2,1)} fusion(f32[6,12,64,64]{2,3,1,0:T(8,128)} %fusion.101, f32[6,12,64,64]{2,3,1,0:T(8,128)} %copy-done.2, f32[6,12,64]{2,1,0:T(8,128)S(1)} %copy-done.15, bf16[6,64,1,12,64]{4,3,2,1,0:T(8,128)(2,1)} %get-tuple-element.142), kind=kOutput, calls=%fused_computation.98 | convolution fusion | flops 39817792 | bytes 3557376 | tf_op jit(solution)/shard_map/nhqk,nkhd->nqhd/dot_general | solution.py:145
  344.6 3.3 convert_reduce_fusion
  348.0 4.7 copy.194
  352.6 6.7 %convert_element_type.160 = bf16[384,2304]{1,0:T(8,128)(2,1)} reshape(bf16[6,64,3,12,64]{4,3,2,1,0:T(8,128)(2,1)} %copy.194) | data formatting | bytes 3538944 | tf_op jit(solution)/shard_map/convert_element_type | solution.py:148
  359.4 4.8 fusion.150
  365.4 2.3 convert_reduce_fusion.4
  369.1 1.8 convolution_convert_fusion.3
  371.2 6.6 %reshape.248 = bf16[384,2304,1,1]{1,0,2,3:T(8,128)(2,1)} reshape(bf16[6,64,3,12,64]{4,3,2,1,0:T(8,128)(2,1)} %copy.194) | data formatting | bytes 3538944 | tf_op jit(solution)/shard_map/convert_element_type | solution.py:148
  377.8 3.6 convolution_convert_fusion.2
  381.4 2.9 pad_maximum_fusion.1.attn_ref
  384.4 4.6 convolution_convert_fusion
  389.0 4.8 convolution_convert_fusion.1
  393.8 8.3 %pad_maximum_fusion.mlp_ref = bf16[2,4,4,48,3072]{4,3,2,1,0:T(8,128)(2,1)} fusion(bf16[1,4,4,48,3072]{4,3,2,1,0:T(8,128)(2,1)} %bitcast.116, bf16[1,4,4,48,3072]{4,3,2,1,0:T(8,128)(2,1)} %bitcast.117), kind=kLoop, calls=%fused_computation.13 | loop fusion | flops 4718592 | bytes 18874368 | tf_op jit(solution)/shard_map/stack | solution.py:159
  403.2 83.2 %scatter_gradients.1 = (f32[6,3072]{1,0:T(8,128)}, f32[2,6,3072]{2,1,0:T(8,128)}, f32[16,768]{1,0:T(8,128)}, f32[8,128]{1,0:T(8,128)}) custom-call(bf16[4,4,48,3072]{3,2,1,0:T(8,128)(2,1)} %pad_maximum_fusion.1.attn_ref, bf16[2,4,4,48,3072]{4,3,2,1,0:T(8,128)(2,1)} %pad_maximum_fusion.mlp_ref, f32[16,768]{1,0:T(8,128)} %pad.10.vector_ref), custom_call_target="tpu_custom_call" | custom-call | tf_op jit(solution)/shard_map/scatter_gradients/pallas_call | solution.py:678
  (222 shorter events, 39.3 us)
Async XLA Ops:
  0.6 88.3 %copy-start.3 = (bf16[1200,768]{1,0:T(8,128)(2,1)S(1)}, bf16[1200,768]{1,0:T(8,128)(2,1)}, u32[]{:S(2)}) copy-start(bf16[1200,768]{1,0:T(8,128)(2,1)} %param.17) | copy-start | bytes 5529604
  87.1 127.3 %copy-start.35 = (f32[768]{0:T(1024)}, f32[768]{0:T(1024)S(1)}, u32[]{:S(2)}) copy-start(f32[768]{0:T(1024)S(1)} %get-tuple-element.109) | copy-start | bytes 9220
  159.6 7.1 %copy-start.4 = (bf16[1200,768]{1,0:T(8,128)(2,1)S(1)}, bf16[1200,768]{1,0:T(8,128)(2,1)}, u32[]{:S(2)}) copy-start(bf16[1200,768]{1,0:T(8,128)(2,1)} %param.17) | copy-start | bytes 5529604
  159.6 7.1 %copy-start.56 = (f32[768]{0:T(1024)S(1)}, f32[768]{0:T(1024)}, u32[]{:S(2)}) copy-start(f32[768]{0:T(1024)} %get-tuple-element.168) | copy-start | bytes 9220
  166.8 5.4 %slice-start.5 = ((f32[12,768]{1,0:T(8,128)}), f32[4,768]{1,0:T(4,128)S(1)}, s32[]{:S(2)}) async-start(f32[12,768]{1,0:T(8,128)} %param.20), calls=%async_computation.5 | async-start | bytes 24576 | tf_op jit(solution)/shard_map/slice | solution.py:85
  204.0 9.9 %copy-start.1 = (bf16[384,768]{1,0:T(8,128)(2,1)S(1)}, bf16[384,768]{1,0:T(8,128)(2,1)}, u32[]{:S(2)}) copy-start(bf16[384,768]{1,0:T(8,128)(2,1)} %param.15) | copy-start | bytes 1769476
  240.2 3.7 copy-start.41
  242.4 72.7 %copy-start.6 = (f32[384,768]{1,0:T(8,128)}, f32[384,768]{1,0:T(8,128)S(1)}, u32[]{:S(2)}) copy-start(f32[384,768]{1,0:T(8,128)S(1)} %get-tuple-element.158) | copy-start | bytes 3538948
  242.5 6.1 %slice-start.2 = ((s8[4718592]{0:T(1024)(128)(4,1)}), s8[4194304]{0:T(1024)(128)(4,1)S(1)}, s32[]{:S(2)}) async-start(s8[4718592]{0:T(1024)(128)(4,1)} %bitcast.113), calls=%async_computation.2 | async-start | bytes 8388608
  243.9 4.7 slice-start.3
  243.9 4.7 copy-start.54
  251.6 54.0 %copy-start.17 = (f32[6,12,64]{2,1,0:T(8,128)S(1)}, f32[6,12,64]{2,1,0:T(8,128)}, u32[]{:S(2)}) copy-start(f32[6,12,64]{2,1,0:T(8,128)} %copy-done.16) | copy-start | bytes 55300
  251.6 54.0 %copy-start.19 = (f32[6,12,64]{2,1,0:T(8,128)S(1)}, f32[6,12,64]{2,1,0:T(8,128)}, u32[]{:S(2)}) copy-start(f32[6,12,64]{2,1,0:T(8,128)} %copy-done.18) | copy-start | bytes 55300
  303.4 11.8 %slice-start = ((s8[4718592]{0:T(1024)(128)(4,1)}), s8[4194304]{0:T(1024)(128)(4,1)S(1)}, s32[]{:S(2)}) async-start(s8[4718592]{0:T(1024)(128)(4,1)} %bitcast.109), calls=%async_computation | async-start | bytes 8388608
  306.2 8.9 %slice-start.1 = ((s8[4718592]{0:T(1024)(128)(4,1)}), s8[524288]{0:T(1024)(128)(4,1)S(1)}, s32[]{:S(2)}) async-start(s8[4718592]{0:T(1024)(128)(4,1)} %bitcast.109), calls=%async_computation.1 | async-start | bytes 1048576
  306.2 8.9 %copy-start.27 = (f32[384]{0:T(512)S(1)}, f32[384]{0:T(512)}, u32[]{:S(2)}) copy-start(f32[384]{0:T(512)} %copy-done.26) | copy-start | bytes 4612
  306.2 8.9 %copy-start.42 = (f32[768]{0:T(1024)S(1)}, f32[768]{0:T(1024)}, u32[]{:S(2)}) copy-start(f32[768]{0:T(1024)} %get-tuple-element.103) | copy-start | bytes 9220
  306.2 8.9 %copy-start.46 = (f32[384]{0:T(512)S(1)}, f32[384]{0:T(512)}, u32[]{:S(2)}) copy-start(f32[384]{0:T(512)} %copy-done.45) | copy-start | bytes 4612
  325.2 3.9 copy-start
  325.2 3.9 copy-start.9
  359.4 4.8 copy-start.32
  359.4 6.0 %copy-start.30 = (f32[384]{0:T(512)S(1)}, f32[384]{0:T(512)}, u32[]{:S(2)}) copy-start(f32[384]{0:T(512)} %copy-done.29) | copy-start | bytes 4612
  359.4 6.0 %copy-start.36 = (f32[768]{0:T(1024)S(1)}, f32[768]{0:T(1024)}, u32[]{:S(2)}) copy-start(f32[768]{0:T(1024)} %copy-done.35) | copy-start | bytes 9220
  377.8 6.5 %slice-start.6 = ((s8[4718592]{0:T(1024)(128)(4,1)}), s8[4194304]{0:T(1024)(128)(4,1)S(1)}, s32[]{:S(2)}) async-start(s8[4718592]{0:T(1024)(128)(4,1)} %bitcast.123), calls=%async_computation.6 | async-start | bytes 8388608
  384.3 4.6 copy-start.7
  384.3 4.6 copy-start.28
  384.3 4.6 copy-start.43
  384.3 4.6 copy-start.47
  384.3 4.6 copy-start.53
  384.3 4.6 copy-start.61
  393.8 8.4 %copy-start.39 = (f32[768]{0:T(1024)S(1)}, f32[768]{0:T(1024)}, u32[]{:S(2)}) copy-start(f32[768]{0:T(1024)} %get-tuple-element.98) | copy-start | bytes 9220
  393.8 8.4 %copy-start.59 = (f32[768]{0:T(1024)S(1)}, f32[768]{0:T(1024)}, u32[]{:S(2)}) copy-start(f32[768]{0:T(1024)} %get-tuple-element.101) | copy-start | bytes 9220
  393.8 8.4 %copy-start.58 = (f32[768]{0:T(1024)S(1)}, f32[768]{0:T(1024)}, u32[]{:S(2)}) copy-start(f32[768]{0:T(1024)} %get-tuple-element.96) | copy-start | bytes 9220
  393.8 8.4 %copy-start.57 = (f32[768]{0:T(1024)S(1)}, f32[768]{0:T(1024)}, u32[]{:S(2)}) copy-start(f32[768]{0:T(1024)} %get-tuple-element.100) | copy-start | bytes 9220
  393.8 8.4 %copy-start.25 = (f32[3,12,64]{2,1,0:T(8,128)S(1)}, f32[3,12,64]{2,1,0:T(8,128)}, u32[]{:S(2)}) copy-start(f32[3,12,64]{2,1,0:T(8,128)} %get-tuple-element.131) | copy-start | bytes 27652
  393.8 8.6 %copy-start.37 = (f32[768]{0:T(1024)S(1)}, f32[768]{0:T(1024)}, u32[]{:S(2)}) copy-start(f32[768]{0:T(1024)} %get-tuple-element.129) | copy-start | bytes 9220
  393.8 8.6 %copy-start.38 = (f32[768]{0:T(1024)S(1)}, f32[768]{0:T(1024)}, u32[]{:S(2)}) copy-start(f32[768]{0:T(1024)} %get-tuple-element.144) | copy-start | bytes 9220
  393.8 8.6 %copy-start.44 = (f32[3072]{0:T(1024)S(1)}, f32[3072]{0:T(1024)}, u32[]{:S(2)}) copy-start(f32[3072]{0:T(1024)} %get-tuple-element.161) | copy-start | bytes 36868
  403.2 86.9 %copy-start.40 = (f32[12,6]{0,1:T(8,128)S(1)}, f32[12,6]{0,1:T(8,128)}, u32[]{:S(2)}) copy-start(f32[12,6]{0,1:T(8,128)} %param.23) | copy-start | bytes 868
  403.2 87.0 %copy-start.50 = (f32[12,6]{0,1:T(8,128)S(1)}, f32[12,6]{0,1:T(8,128)}, u32[]{:S(2)}) copy-start(f32[12,6]{0,1:T(8,128)} %param.29) | copy-start | bytes 868
  403.2 87.1 %copy-start.51 = (f32[12,6]{0,1:T(8,128)S(1)}, f32[12,6]{0,1:T(8,128)}, u32[]{:S(2)}) copy-start(f32[12,6]{0,1:T(8,128)} %param.26) | copy-start | bytes 868
  403.2 88.7 %copy-start.13 = (f32[6,3072]{1,0:T(8,128)S(1)}, f32[6,3072]{1,0:T(8,128)}, u32[]{:S(2)}) copy-start(f32[6,3072]{1,0:T(8,128)} %attn_ref.1) | copy-start | bytes 221188
  403.2 88.7 %copy-start.23 = (f32[6,3072]{1,0:T(8,128)S(1)}, f32[6,3072]{1,0:T(8,128)}, u32[]{:S(2)}) copy-start(f32[6,3072]{1,0:T(8,128)} %param.27) | copy-start | bytes 221188
  403.2 88.7 %copy-start.24 = (f32[6,3072]{1,0:T(8,128)S(1)}, f32[6,3072]{1,0:T(8,128)}, u32[]{:S(2)}) copy-start(f32[6,3072]{1,0:T(8,128)} %param.24) | copy-start | bytes 221188
  403.2 90.3 %copy-start.12 = (f32[2,6,3072]{2,0,1:T(2,128)S(1)}, f32[2,6,3072]{2,0,1:T(2,128)}, u32[]{:S(2)}) copy-start(f32[2,6,3072]{2,0,1:T(2,128)} %param.22) | copy-start | bytes 442372
  403.2 90.3 %copy-start.21 = (f32[2,6,3072]{2,0,1:T(2,128)S(1)}, f32[2,6,3072]{2,0,1:T(2,128)}, u32[]{:S(2)}) copy-start(f32[2,6,3072]{2,0,1:T(2,128)} %param.28) | copy-start | bytes 442372
  403.2 90.3 %copy-start.22 = (f32[2,6,3072]{2,0,1:T(2,128)S(1)}, f32[2,6,3072]{2,0,1:T(2,128)}, u32[]{:S(2)}) copy-start(f32[2,6,3072]{2,0,1:T(2,128)} %param.25) | copy-start | bytes 442372
  486.4 12.7 %copy-start.14 = (f32[6,3072]{1,0:T(8,128)S(1)}, f32[6,3072]{1,0:T(8,128)}, u32[]{:S(2)}) copy-start(f32[6,3072]{1,0:T(8,128)} %get-tuple-element.187) | copy-start | bytes 221188
  (23 other events, 45.0 us)
